TPU v7x, 256 devices: a whole 4x4x8 slice. The times are simulated.
256 devices in a mesh: row: 2 (over core), col: 4 (over x), vis: 32 (over z, y).
Axes of the slice: x: 4, y: 4, z: 8, core: 2. Of those that a mesh axis runs over, the one named last changes fastest.
Arguments:
- text_embed: bfloat16 [32, 256, 5120], P('vis', None, 'row'), may hold values from -6 to 6
- image_embed: bfloat16 [32, 64, 5120], P('vis', 'col', 'row'), may hold values from -6 to 6
- slot_source: int32 [32, 256], replicated, may hold values from -1 to 2047, as said below
- segment_ids: int32 [32, 256], P('vis'), may hold values from 0 to 3, never falling along the last dimension, each value on 1 to 128 neighbouring positions
- prefix_lengths: int32 [32, 4], P('vis'), may hold values from 1 to 1024, 2048 in all within a row
- attn_gain: float32 [5120], P('row'), may hold values from 0.1 to 1.9
- qkv_weight: bfloat16 [5120, 3, 5120], P('row', None, 'col'), may hold values from -0.64286954 to 0.64286954
- out_weight: bfloat16 [5120, 5120], P('col', 'row'), may hold values from -0.5 to 0.5
- cache_keys: bfloat16 [32, 4, 1024, 5120], P('vis', None, 'row', 'col'), may hold values from -48 to 48
- cache_values: bfloat16 [32, 4, 1024, 5120], P('vis', None, 'row', 'col'), may hold values from -6 to 6
Outputs:
- hidden: float32 [32, 256, 5120], P('vis', 'col', 'row')
- new_keys: float32 [32, 256, 5120], P('vis', 'row', 'col')
- new_values: float32 [32, 256, 5120], P('vis', 'row', 'col')
- request_rms: float32 [32, 4], P('vis')
Inputs may be any that keep to these rules, and one draw needn't show every extreme that they name: `slot_source`: every global image index appears in exactly one slot; all other slots hold -1. The image tokens of one producing group fill at most 4 slots of any one group, and in every draw some group holds exactly 4 image tokens of every producing group.
All inputs are finite; a program needn't handle non-finite values.
Results may differ from a plain program's by a relative error of at most 0.012.
The roundings to bfloat16 on the way count: a program that leaves them out, or rounds other values in their place, can miss the bound.
Values may be sent and summed in bfloat16 or wider, within the bound.
A program may use at most 192 MiB of HBM per device.

v0:
```python
import jax
import jax.numpy as jnp
from jax import lax
from jax.sharding import PartitionSpec as P

D = 5120
HD = 128
EPSILON = 1e-06


def combined_all(value, axis, join):
    pieces = jax.tree.map(lambda part: lax.all_gather(part, axis), value)
    head = jax.tree.map(lambda part: part[0], pieces)
    tail = jax.tree.map(lambda part: part[1:], pieces)
    running, _ = lax.scan(lambda running, slab: (join(running, slab), None), head, tail)
    return running


def combine_parts(earlier_part, later_part):
    earlier_peak, earlier_sum, earlier_acc = earlier_part
    later_peak, later_sum, later_acc = later_part
    joint_peak = jnp.maximum(earlier_peak, later_peak)
    earlier_factor = jnp.exp(earlier_peak - joint_peak)
    later_factor = jnp.exp(later_peak - joint_peak)
    joint_sum = earlier_sum * earlier_factor + later_sum * later_factor
    joint_acc = earlier_acc * earlier_factor[..., None] + later_acc * later_factor[..., None]
    return (joint_peak, joint_sum, joint_acc)


def attend_block(queries, key_rows, value_rows, allowed):
    scores = jnp.einsum(
        "thd,khd->htk", queries, key_rows, preferred_element_type=jnp.float32
    ) * HD ** (-0.5)
    masked = jnp.where(allowed[None], scores, -1e30)
    peak_score = jnp.max(masked, axis=2)
    weights = jnp.where(allowed[None], jnp.exp(masked - peak_score[..., None]), 0.0)
    weight_sum = jnp.sum(weights, axis=2)
    summed = jnp.einsum(
        "htk,khd->htd", weights.astype(jnp.bfloat16), value_rows, preferred_element_type=jnp.float32
    )
    return (peak_score, weight_sum, summed)


def per_device(
    text_embed,
    image_embed,
    slot_source,
    segment_ids,
    prefix_lengths,
    attn_gain,
    qkv_weight,
    out_weight,
    cache_keys,
    cache_values,
):
    row_count = lax.axis_size("row")
    col_count = lax.axis_size("col")
    vis_count = lax.axis_size("vis")
    row_index = lax.axis_index("row")
    col_index = lax.axis_index("col")
    vis_index = lax.axis_index("vis")
    text_rows = text_embed[0]
    tokens_here = text_rows.shape[0]
    feature_width = text_rows.shape[1]
    sources = lax.dynamic_index_in_dim(slot_source, vis_index, 0, keepdims=False)
    pieces = lax.all_gather(image_embed, ("col", "vis"), axis=0, tiled=True)
    per_piece = pieces.shape[1]
    flat_rows = pieces.reshape(-1, feature_width)
    safe_index = jnp.maximum(sources, 0)
    group_size = per_piece * col_count
    group_of = safe_index // group_size
    within = safe_index % group_size
    located = (within // per_piece * vis_count + group_of) * per_piece + within % per_piece
    picked_rows = jnp.take(flat_rows, located, axis=0)
    filled = jnp.where((sources >= 0)[:, None], picked_rows, text_rows)
    wide_rows = filled.astype(jnp.float32)
    square_part = jnp.sum(wide_rows * wide_rows, axis=1)
    scaled = (wide_rows * attn_gain).astype(jnp.bfloat16)
    projected = jnp.einsum("td,dkh->tkh", scaled, qkv_weight, preferred_element_type=jnp.float32)
    blocks = tokens_here // row_count
    summed_all, square_sums = lax.psum((projected, square_part), "row")
    inv_rms = lax.rsqrt(square_sums / D + EPSILON)
    queries = (summed_all[:, 0] * inv_rms[:, None]).astype(jnp.bfloat16)
    pair_normed = summed_all[:, 1:] * inv_rms[:, None, None]
    pair_exact = lax.dynamic_slice_in_dim(pair_normed, row_index * blocks, blocks, 0)
    pair_mine = pair_exact.astype(jnp.bfloat16)
    head_width = queries.shape[1]
    heads_here = head_width // HD
    segments = segment_ids[0]
    lengths = prefix_lengths[0]
    request_count = lengths.shape[0]
    cache_block = cache_keys.shape[2]
    request_ids = jnp.arange(request_count, dtype=jnp.int32)
    cache_request = jnp.repeat(request_ids, cache_block)
    cache_position = row_index * cache_block + jnp.tile(
        jnp.arange(cache_block, dtype=jnp.int32), request_count
    )
    cache_ok = (cache_request[None, :] == segments[:, None]) & (
        cache_position < lengths[cache_request]
    )[None, :]
    token_ids = jnp.arange(tokens_here, dtype=jnp.int32)
    block_ids = row_index * blocks + jnp.arange(blocks, dtype=jnp.int32)
    block_segments = lax.dynamic_slice_in_dim(segments, row_index * blocks, blocks, 0)
    prompt_ok = (block_segments[None, :] == segments[:, None]) & (
        block_ids[None, :] <= token_ids[:, None]
    )
    allowed = jnp.concatenate([cache_ok, prompt_ok], axis=1)
    key_rows = jnp.concatenate(
        [cache_keys[0].reshape(-1, head_width), pair_mine[:, 0]], axis=0
    ).reshape(-1, heads_here, HD)
    value_rows = jnp.concatenate(
        [cache_values[0].reshape(-1, head_width), pair_mine[:, 1]], axis=0
    ).reshape(-1, heads_here, HD)
    local_parts = attend_block(
        queries.reshape(tokens_here, heads_here, HD), key_rows, value_rows, allowed
    )
    peak_score, weight_sum, summed = combined_all(local_parts, "row", combine_parts)
    attended = (
        (summed / weight_sum[..., None])
        .transpose(1, 0, 2)
        .reshape(tokens_here, head_width)
        .astype(jnp.bfloat16)
    )
    update = jnp.dot(attended, out_weight, preferred_element_type=jnp.float32)
    shares = lax.psum_scatter(update, "col", scatter_dimension=0, tiled=True)
    share_rows = tokens_here // col_count
    residual = lax.dynamic_slice_in_dim(wide_rows, col_index * share_rows, share_rows, 0)
    hidden = residual + shares
    onehot = (segments[None, :] == request_ids[:, None]).astype(jnp.float32)
    totals = jnp.dot(onehot, square_sums, precision=lax.Precision.HIGHEST)
    counts = jnp.sum(onehot, axis=1)
    request_rms = jnp.sqrt(totals / (counts * D))
    return (hidden[None], pair_exact[:, 0][None], pair_exact[:, 1][None], request_rms[None])


def solution(mesh):
    return jax.shard_map(
        per_device,
        mesh=mesh,
        in_specs=(
            P("vis", None, "row"),
            P("vis", "col", "row"),
            P(),
            P("vis", None),
            P("vis", None),
            P("row"),
            P("row", None, "col"),
            P("col", "row"),
            P("vis", None, "row", "col"),
            P("vis", None, "row", "col"),
        ),
        out_specs=(
            P("vis", "col", "row"),
            P("vis", "row", "col"),
            P("vis", "row", "col"),
            P("vis", None),
        ),
        check_vma=False,
    )
```

profile of v0, /device:TPU:1, one launch (start us, length us, event | category | flops | bytes accessed | tf_op | source)
XLA Modules:
  0.0 334.3 jit_solution(8110566947763616634)
XLA Ops:
  10.1 134.3 %all-gather.8.cloned.1.call-done = bf16[128,16,2560]{2,1,0:T(8,128)(2,1)} async-done(((bf16[1,16,2560]{2,1,0:T(8,128)(2,1)}), bf16[128,16,2560]{2,1,0:T(8,128)(2,1)}) %all-gather.8.cloned.1.call-update) | async-done | bytes 10485776 | tf_op jit(solution)/shard_map/all_gather | solution.py:66
  144.5 9.1 %gather_fusion = bf16[256,2560]{1,0:T(8,128)(2,1)} fusion(bf16[2048,2560]{1,0:T(8,128)(2,1)} %bitcast.111, s32[1024]{0:T(1024)S(1)} %pad_clamp_fusion), kind=kCustom, calls=%fused_computation | custom fusion | bytes 2622464 | tf_op jit(solution)/shard_map/jit(_take)/gather | solution.py:74
  153.6 2.4 multiply_reduce_fusion
  156.0 11.2 %fusion.14 = f32[256,3,1280]{2,0,1:T(8,128)} fusion(bf16[2560,3,1280]{2,0,1:T(8,128)(2,1)} %param.16, f32[256,2560]{1,0:T(8,128)S(1)} %get-tuple-element.33, f32[2560]{0:T(1024)S(1)} %copy-done.1), kind=kOutput, calls=%fused_computation.20 | convolution fusion | flops 5034475520 | bytes 26224640 | tf_op jit(solution)/shard_map/td,dkh->tkh/dot_general | solution.py:79
  167.4 11.3 %reshape.366 = bf16[2048,10,128]{2,1,0:T(8,128)(2,1)} reshape(bf16[1,4,512,1280]{3,2,1,0:T(8,128)(2,1)} %param.18) | data formatting | bytes 10485760 | tf_op jit(solution)/shard_map/concatenate | solution.py:108
  178.7 7.5 %copy.43 = bf16[2048,10,128]{2,0,1:T(8,128)(2,1)} copy(bf16[2048,10,128]{2,1,0:T(8,128)(2,1)} %reshape.366) | data formatting | bytes 10485760 | tf_op jit(solution)/shard_map/concatenate | solution.py:108
  186.2 11.3 %reshape.367 = bf16[2048,10,128]{2,1,0:T(8,128)(2,1)} reshape(bf16[1,4,512,1280]{3,2,1,0:T(8,128)(2,1)} %param.19) | data formatting | bytes 10485760 | tf_op jit(solution)/shard_map/concatenate | solution.py:111
  197.5 7.7 %copy.48 = bf16[2048,10,128]{2,0,1:T(8,128)(2,1)} copy(bf16[2048,10,128]{2,1,0:T(8,128)(2,1)} %reshape.367) | data formatting | bytes 10485760 | tf_op jit(solution)/shard_map/concatenate | solution.py:111
  205.8 2.6 compare_select_fusion.1
  209.0 3.4 %psum.15 = f32[256]{0:T(256)S(1)} all-reduce(f32[256]{0:T(256)S(1)} %get-tuple-element.32), channel_id=1, replica_groups=mesh['row'=2,'col'=4,'vis'=32] {'row'}, use_global_device_ids=true, to_apply=%region_2.3 | all-reduce | flops 256 | bytes 2048 | tf_op jit(solution)/shard_map/psum | solution.py:81
  212.5 2.5 slice.70
  215.0 2.8 copy.40
  217.8 1.7 slice-done
  219.5 1.3 fusion.42
  220.8 0.8 fusion.45
  221.6 1.9 copy.47
  223.5 1.9 copy.49
  225.3 0.9 copy.42
  226.2 1.2 copy.44
  227.4 14.4 %fusion = (f32[10,256]{1,0:T(8,128)S(1)}, f32[10,256,2176]{2,1,0:T(8,128)}) fusion(pred[256,2176]{1,0:T(8,128)(4,1)S(1)} %pad_add_fusion, bf16[128,10,128]{2,0,1:T(8,128)(2,1)S(1)} %copy.44, bf16[2048,10,128]{2,0,1:T(8,128)(2,1)} %copy.43, f32[256,10,128]{0,2,1:T(8,128)} %bitcast.113, f32[256]{0:T(256)S(1)} %add_rsqrt_fusion), kind=kOutput, calls=%fused_computation.3 | convolution fusion | flops 1454568960 | bytes 29731840 | tf_op jit(solution)/shard_map/thd,khd->htk/dot_general | solution.py:31
  241.8 13.0 %fusion.3 = f32[10,256,128]{2,1,0:T(8,128)} fusion(f32[10,256,2176]{2,1,0:T(8,128)} %get-tuple-element.47, f32[10,256]{1,0:T(8,128)S(1)} %get-tuple-element.46, pred[256,2176]{1,0:T(8,128)(4,1)S(1)} %pad_add_fusion, bf16[128,10,128]{2,0,1:T(8,128)(2,1)S(1)} %copy-done, bf16[2048,10,128]{2,0,1:T(8,128)(2,1)} %copy.48), kind=kOutput, calls=%fused_computation.6 | convolution fusion | flops 1465057280 | bytes 29730816 | tf_op jit(solution)/shard_map/htk,khd->htd/dot_general | solution.py:38
  254.9 1.8 all-gather.3
  256.8 11.7 %fusion.1 = f32[10,256]{1,0:T(8,128)S(1)} fusion(f32[10,256,2176]{2,1,0:T(8,128)} %get-tuple-element.47, f32[10,256]{1,0:T(8,128)S(1)} %get-tuple-element.46, pred[256,2176]{1,0:T(8,128)(4,1)S(1)} %pad_add_fusion), kind=kLoop, calls=%fused_computation.4 | loop fusion | flops 27850240 | bytes 22859776 | tf_op jit(solution)/shard_map/reduce_sum | solution.py:37
  268.5 2.1 all-gather.4
  271.2 3.5 %fusion.44 = (f32[10,256,128]{2,1,0:T(8,128)}, f32[10,256,128]{2,1,0:T(8,128)}) fusion(f32[20,256,128]{2,1,0:T(8,128)} %all-gather.10.cloned.1.call-done), kind=kLoop, calls=%fused_computation.97 | loop fusion | bytes 5242880 | tf_op jit(solution)/shard_map/slice | solution.py:13
  274.7 2.8 copy.57
  277.5 2.8 copy.58
  280.3 2.0 divide_convert_fusion
  282.2 6.3 %fusion.47 = f32[256,2560]{1,0:T(8,128)} fusion(bf16[256,1280]{0,1:T(8,128)(2,1)S(1)} %bitcast.112, bf16[1280,2560]{1,0:T(8,128)(2,1)} %param.17), kind=kOutput, calls=%fused_computation.100 | convolution fusion | flops 1677721600 | bytes 9830400 | tf_op jit(solution)/shard_map/dot_general | solution.py:124
  289.3 2.4 slice_bitcast_fusion
  291.7 34.1 %reduce-scatter.2.cloned.1.call-done = f32[64,2560]{1,0:T(8,128)} async-done(((f32[256,2560]{1,0:T(8,128)}), f32[64,2560]{1,0:T(8,128)}) %reduce-scatter.2.cloned.1.call-update) | async-done | bytes 655376 | tf_op jit(solution)/shard_map/reduce_scatter | solution.py:125
  325.8 2.0 add_bitcast_fusion
  (42 shorter events, 5.8 us)
Async XLA Ops:
  7.2 137.3 %all-gather.8.cloned.1.call-start = ((), (), s32[]{:S(2)}) async-start(), calls=%async_computation.1 | async-start | bytes 10567680 | tf_op jit(solution)/shard_map/all_gather | solution.py:66
  7.9 204.6 %all-reduce.2.cloned.1.call-start = ((), (), s32[]{:S(2)}) async-start(), calls=%async_computation.2 | async-start | bytes 7864320 | tf_op jit(solution)/shard_map/psum | solution.py:81
  153.6 2.4 copy-start.1
  167.2 104.0 %all-gather.10.cloned.1.call-start = ((), (), s32[]{:S(2)}) async-start(), calls=%async_computation.4 | async-start | bytes 3932160 | tf_op jit(solution)/shard_map/all_gather | solution.py:12
  197.5 7.7 %copy-start.2 = (s32[1,4]{1,0:T(1,128)S(1)}, s32[1,4]{1,0:T(1,128)}, u32[]{:S(2)}) copy-start(s32[1,4]{1,0:T(1,128)} %param.14) | copy-start | bytes 52
  197.5 10.9 %copy-start.3 = (s32[1,256]{1,0:T(1,128)S(1)}, s32[1,256]{1,0:T(1,128)}, u32[]{:S(2)}) copy-start(s32[1,256]{1,0:T(1,128)} %param.13) | copy-start | bytes 3076
  217.8 1.7 slice-start
  227.4 14.4 %copy-start = (bf16[128,10,128]{2,0,1:T(8,128)(2,1)S(1)}, bf16[128,10,128]{2,0,1:T(8,128)(2,1)}, u32[]{:S(2)}) copy-start(bf16[128,10,128]{2,0,1:T(8,128)(2,1)} %copy.49) | copy-start | bytes 983044
  254.9 70.9 %reduce-scatter.2.cloned.1.call-start = ((), (), s32[]{:S(2)}) async-start(), calls=%async_computation.3 | async-start | bytes 3276800 | tf_op jit(solution)/shard_map/reduce_scatter | solution.py:125
Sparse Core Ops, SparseCore 0:
  11.5 132.9 all-gather.7
  167.4 33.9 all-reduce.1
  255.0 16.1 all-gather.9
  288.6 37.0 reduce-scatter.1
where the time goes:
time: 336 us; the launch traced here: 334 us
  waiting for transfers between devices  170 us (51%)
  local copies, waits for them, and re-layouts  72.7 us (22%)
  matrix products  45.5 us (14%)
  other arithmetic  24.8 us (7%)
  between operations  13.9 us (4%)
  blocking collectives  7.32 us (2%)
    all_gather x1, waiting for transfers between devices, per_device(): pieces = lax.all_gather(image_embed, ('col', 'vis'), axis=0, tiled=True)  134 us
    reduce_scatter x1, waiting for transfers between devices, per_device(): shares = lax.psum_scatter(update, 'col', scatter_dimension=0, tiled=True)  34.1 us
    concatenate x3, local copies, waits for them, and re-layouts, per_device(): jnp.concatenate([cache_values[0].reshape(-1, head_width), pair_mine[:, 1]...  20.8 us
    concatenate x3, local copies, waits for them, and re-layouts, per_device(): jnp.concatenate([cache_keys[0].reshape(-1, head_width), pair_mine[:, 0]],...  20 us
    dot_general x1, matrix products, attend_block(): jnp.einsum('thd,khd->htk', queries, key_rows, preferred_element_type=jnp....  14.4 us
    dot_general x1, matrix products, attend_block(): jnp.einsum('htk,khd->htd', weights.astype(jnp.bfloat16), value_rows, pref...  13 us
    reduce_sum x1, other arithmetic, attend_block(): weight_sum = jnp.sum(weights, axis=2)  11.7 us
    dot_general x1, matrix products, per_device(): jnp.einsum('td,dkh->tkh', scaled, qkv_weight, preferred_element_type=jnp....  11.2 us
  transfers between devices with their start and end apart: 4, of which 3 were waited for; matrix products, arithmetic and copies ran while one was open for 18% of the time, Pallas kernels for 0%

commit v1 on v0

--- a/solution.py
+++ b/solution.py
@@ -63,7 +63,16 @@
     tokens_here = text_rows.shape[0]
     feature_width = text_rows.shape[1]
     sources = lax.dynamic_index_in_dim(slot_source, vis_index, 0, keepdims=False)
-    pieces = lax.all_gather(image_embed, ("col", "vis"), axis=0, tiled=True)
+
+    def tell_slices_here(xin, peer_axis):
+        return jnp.concatenate(
+            lax.all_to_all(
+                jnp.stack([xin for _ in range(lax.axis_size(peer_axis))]), peer_axis, 0, 0
+            ),
+            axis=0,
+        )
+
+    pieces = tell_slices_here(image_embed, ("col", "vis"))
     per_piece = pieces.shape[1]
     flat_rows = pieces.reshape(-1, feature_width)
     safe_index = jnp.maximum(sources, 0)

time: 336 us -> 450 us (1.34)
  waiting for transfers between devices: 170 us -> 256 us
  starting transfers between devices: 0.16 us -> 17.1 us
  local copies, waits for them, and re-layouts: 72.7 us -> 79.3 us
    all_to_all x0 -> x1, waiting for transfers between devices: none -> 225 us  [tell_slices_here(): lax.all_to_all(jnp.stack([xin for _ in range(lax.axis_size(peer_axis))]),...]
    all_gather x1 -> x0, waiting for transfers between devices: 134 us -> none  [per_device(): pieces = lax.all_gather(image_embed, ('col', 'vis'), axis=0, tiled=True)]
    all_to_all x0 -> x1, starting transfers between devices: none -> 16.8 us  [tell_slices_here(): lax.all_to_all(jnp.stack([xin for _ in range(lax.axis_size(peer_axis))]),...]
    another operation x0 -> x1, local copies, waits for them, and re-layouts: none -> 6.02 us  [tell_slices_here(): jnp.stack([xin for _ in range(lax.axis_size(peer_axis))])]
  transfers between devices with their start and end apart: 4 -> 4, of which waited for: 3 -> 2; matrix products, arithmetic and copies ran while one was open for 18% -> 13% of each run, Pallas kernels for 0% -> 0%
where the time goes in v1:
time: 450 us; the launch traced here: 448 us
  waiting for transfers between devices  256 us (57%)
  local copies, waits for them, and re-layouts  79.3 us (18%)
  matrix products  45.7 us (10%)
  other arithmetic  25.1 us (6%)
  starting transfers between devices  17.1 us (4%)
  between operations  13.9 us (3%)
  blocking collectives  11 us (2%)
    all_to_all x1, waiting for transfers between devices, tell_slices_here(): lax.all_to_all(jnp.stack([xin for _ in range(lax.axis_size(peer_axis))]),...  225 us
    reduce_scatter x1, waiting for transfers between devices, per_device(): shares = lax.psum_scatter(update, 'col', scatter_dimension=0, tiled=True)  30.9 us
    concatenate x3, local copies, waits for them, and re-layouts, per_device(): jnp.concatenate([cache_values[0].reshape(-1, head_width), pair_mine[:, 1]...  21.6 us
    concatenate x3, local copies, waits for them, and re-layouts, per_device(): jnp.concatenate([cache_keys[0].reshape(-1, head_width), pair_mine[:, 0]],...  19.8 us
    all_to_all x1, starting transfers between devices, tell_slices_here(): lax.all_to_all(jnp.stack([xin for _ in range(lax.axis_size(peer_axis))]),...  16.8 us
    dot_general x1, matrix products, attend_block(): jnp.einsum('thd,khd->htk', queries, key_rows, preferred_element_type=jnp....  14.5 us
    dot_general x1, matrix products, attend_block(): jnp.einsum('htk,khd->htd', weights.astype(jnp.bfloat16), value_rows, pref...  13 us
    reduce_sum x1, other arithmetic, attend_block(): weight_sum = jnp.sum(weights, axis=2)  12 us
  transfers between devices with their start and end apart: 4, of which 2 were waited for; matrix products, arithmetic and copies ran while one was open for 13% of the time, Pallas kernels for 0%

profile of v1, /device:TPU:1, one launch (start us, length us, event | category | flops | bytes accessed | tf_op | source)
XLA Modules:
  0.0 448.0 jit_solution(15001932974803149367)
XLA Ops:
  7.2 6.0 %stack.2 = bf16[128,1,16,2560]{3,2,1,0:T(8,128)(2,1)} broadcast(bf16[16,2560]{1,0:T(8,128)(2,1)} %bitcast.116), dimensions={2,3} | broadcast | bytes 10567680 | tf_op jit(solution)/shard_map/stack | solution.py:70
  13.2 16.8 %all-to-all-start = ((bf16[128,1,16,2560]{3,2,1,0:T(8,128)(2,1)}), bf16[128,1,16,2560]{3,2,1,0:T(8,128)(2,1)}, u32[]{:S(2)}, u32[]{:S(2)}) async-start(bf16[128,1,16,2560]{3,2,1,0:T(8,128)(2,1)} %stack.2), calls=%async_computation | async-start | bytes 20971520 | tf_op jit(solution)/shard_map/all_to_all | solution.py:69
  32.2 224.9 %all-to-all-done = bf16[128,1,16,2560]{3,2,1,0:T(8,128)(2,1)} async-done(((bf16[128,1,16,2560]{3,2,1,0:T(8,128)(2,1)}), bf16[128,1,16,2560]{3,2,1,0:T(8,128)(2,1)}, u32[]{:S(2)}, u32[]{:S(2)}) %all-to-all-start) | async-done | bytes 10485792 | tf_op jit(solution)/shard_map/all_to_all | solution.py:69
  257.1 9.1 %gather_fusion = bf16[256,2560]{1,0:T(8,128)(2,1)} fusion(bf16[2048,2560]{1,0:T(8,128)(2,1)} %bitcast.3, s32[1024]{0:T(1024)S(1)} %pad_clamp_fusion), kind=kCustom, calls=%fused_computation | custom fusion | bytes 2622464 | tf_op jit(solution)/shard_map/jit(_take)/gather | solution.py:83
  266.3 2.4 multiply_reduce_fusion
  268.7 11.2 %fusion.14 = f32[256,3,1280]{2,0,1:T(8,128)} fusion(bf16[2560,3,1280]{2,0,1:T(8,128)(2,1)} %param.16, f32[256,2560]{1,0:T(8,128)S(1)} %get-tuple-element.33, f32[2560]{0:T(1024)S(1)} %copy-done.1), kind=kOutput, calls=%fused_computation.20 | convolution fusion | flops 5034475520 | bytes 26224640 | tf_op jit(solution)/shard_map/td,dkh->tkh/dot_general | solution.py:88
  280.2 11.3 %reshape.365 = bf16[2048,10,128]{2,1,0:T(8,128)(2,1)} reshape(bf16[1,4,512,1280]{3,2,1,0:T(8,128)(2,1)} %param.18) | data formatting | bytes 10485760 | tf_op jit(solution)/shard_map/concatenate | solution.py:117
  291.5 7.3 %copy.43 = bf16[2048,10,128]{2,0,1:T(8,128)(2,1)} copy(bf16[2048,10,128]{2,1,0:T(8,128)(2,1)} %reshape.365) | data formatting | bytes 10485760 | tf_op jit(solution)/shard_map/concatenate | solution.py:117
  298.8 11.3 %reshape.366 = bf16[2048,10,128]{2,1,0:T(8,128)(2,1)} reshape(bf16[1,4,512,1280]{3,2,1,0:T(8,128)(2,1)} %param.19) | data formatting | bytes 10485760 | tf_op jit(solution)/shard_map/concatenate | solution.py:120
  310.1 8.5 %copy.48 = bf16[2048,10,128]{2,0,1:T(8,128)(2,1)} copy(bf16[2048,10,128]{2,1,0:T(8,128)(2,1)} %reshape.366) | data formatting | bytes 10485760 | tf_op jit(solution)/shard_map/concatenate | solution.py:120
  319.2 2.6 compare_select_fusion.1
  322.4 7.0 %psum.15 = f32[256]{0:T(256)S(1)} all-reduce(f32[256]{0:T(256)S(1)} %get-tuple-element.32), channel_id=1, replica_groups=mesh['row'=2,'col'=4,'vis'=32] {'row'}, use_global_device_ids=true, to_apply=%region_2.3 | all-reduce | flops 256 | bytes 2048 | tf_op jit(solution)/shard_map/psum | solution.py:90
  329.5 2.5 slice.70
  332.0 2.8 copy.40
  334.8 1.7 slice-done
  336.5 1.3 fusion.42
  338.6 1.9 copy.47
  340.4 1.9 copy.49
  343.2 1.2 copy.44
  344.4 14.5 %fusion = (f32[10,256]{1,0:T(8,128)S(1)}, f32[10,256,2176]{2,1,0:T(8,128)}) fusion(pred[256,2176]{1,0:T(8,128)(4,1)S(1)} %pad_add_fusion, bf16[128,10,128]{2,0,1:T(8,128)(2,1)S(1)} %copy.44, bf16[2048,10,128]{2,0,1:T(8,128)(2,1)} %copy.43, f32[256,10,128]{0,2,1:T(8,128)} %bitcast.113, f32[256]{0:T(256)S(1)} %add_rsqrt_fusion), kind=kOutput, calls=%fused_computation.3 | convolution fusion | flops 1454568960 | bytes 29731840 | tf_op jit(solution)/shard_map/thd,khd->htk/dot_general | solution.py:31
  358.9 13.0 %fusion.3 = f32[10,256,128]{2,1,0:T(8,128)} fusion(f32[10,256,2176]{2,1,0:T(8,128)} %get-tuple-element.47, f32[10,256]{1,0:T(8,128)S(1)} %get-tuple-element.46, pred[256,2176]{1,0:T(8,128)(4,1)S(1)} %pad_add_fusion, bf16[128,10,128]{2,0,1:T(8,128)(2,1)S(1)} %copy-done, bf16[2048,10,128]{2,0,1:T(8,128)(2,1)} %copy.48), kind=kOutput, calls=%fused_computation.6 | convolution fusion | flops 1465057280 | bytes 29730816 | tf_op jit(solution)/shard_map/htk,khd->htd/dot_general | solution.py:38
  372.1 1.8 all-gather.3
  373.9 12.0 %fusion.1 = f32[10,256]{1,0:T(8,128)S(1)} fusion(f32[10,256,2176]{2,1,0:T(8,128)} %get-tuple-element.47, f32[10,256]{1,0:T(8,128)S(1)} %get-tuple-element.46, pred[256,2176]{1,0:T(8,128)(4,1)S(1)} %pad_add_fusion), kind=kLoop, calls=%fused_computation.4 | loop fusion | flops 27850240 | bytes 22859776 | tf_op jit(solution)/shard_map/reduce_sum | solution.py:37
  385.9 2.1 all-gather.4
  388.1 3.5 fusion.44
  391.6 2.8 copy.57
  394.4 2.8 copy.58
  397.1 2.0 divide_convert_fusion
  399.1 6.3 %fusion.47 = f32[256,2560]{1,0:T(8,128)} fusion(bf16[256,1280]{0,1:T(8,128)(2,1)S(1)} %bitcast.112, bf16[1280,2560]{1,0:T(8,128)(2,1)} %param.17), kind=kOutput, calls=%fused_computation.100 | convolution fusion | flops 1677721600 | bytes 9830400 | tf_op jit(solution)/shard_map/dot_general | solution.py:133
  406.2 2.4 slice_bitcast_fusion
  408.6 30.9 %reduce-scatter.2.cloned.1.call-done = f32[64,2560]{1,0:T(8,128)} async-done(((f32[256,2560]{1,0:T(8,128)}), f32[64,2560]{1,0:T(8,128)}) %reduce-scatter.2.cloned.1.call-update) | async-done | bytes 655376 | tf_op jit(solution)/shard_map/reduce_scatter | solution.py:134
  439.4 2.0 add_bitcast_fusion
  (42 shorter events, 6.3 us)
Async XLA Ops:
  13.2 243.9 %all-to-all-start = ((bf16[128,1,16,2560]{3,2,1,0:T(8,128)(2,1)}), bf16[128,1,16,2560]{3,2,1,0:T(8,128)(2,1)}, u32[]{:S(2)}, u32[]{:S(2)}) async-start(bf16[128,1,16,2560]{3,2,1,0:T(8,128)(2,1)} %stack.2), calls=%async_computation | async-start | bytes 20971520 | tf_op jit(solution)/shard_map/all_to_all | solution.py:69
  30.0 299.5 %all-reduce.2.cloned.1.call-start = ((), (), s32[]{:S(2)}) async-start(), calls=%async_computation.2 | async-start | bytes 7864320 | tf_op jit(solution)/shard_map/psum | solution.py:90
  266.3 2.4 copy-start.1
  279.9 108.1 %all-gather.7.cloned.1.call-start = ((), (), s32[]{:S(2)}) async-start(), calls=%async_computation.4 | async-start | bytes 3932160 | tf_op jit(solution)/shard_map/all_gather | solution.py:12
  310.1 8.5 %copy-start.2 = (s32[1,4]{1,0:T(1,128)S(1)}, s32[1,4]{1,0:T(1,128)}, u32[]{:S(2)}) copy-start(s32[1,4]{1,0:T(1,128)} %param.14) | copy-start | bytes 52
  310.1 11.7 %copy-start.3 = (s32[1,256]{1,0:T(1,128)S(1)}, s32[1,256]{1,0:T(1,128)}, u32[]{:S(2)}) copy-start(s32[1,256]{1,0:T(1,128)} %param.13) | copy-start | bytes 3076
  334.8 1.7 slice-start
  344.4 14.5 %copy-start = (bf16[128,10,128]{2,0,1:T(8,128)(2,1)S(1)}, bf16[128,10,128]{2,0,1:T(8,128)(2,1)}, u32[]{:S(2)}) copy-start(bf16[128,10,128]{2,0,1:T(8,128)(2,1)} %copy.49) | copy-start | bytes 983044
  372.0 67.4 %reduce-scatter.2.cloned.1.call-start = ((), (), s32[]{:S(2)}) async-start(), calls=%async_computation.3 | async-start | bytes 3276800 | tf_op jit(solution)/shard_map/reduce_scatter | solution.py:134
Sparse Core Ops, SparseCore 0:
  280.0 35.6 all-reduce.1
  372.1 12.6 all-gather.6
  405.5 33.8 reduce-scatter.1
